TPU v7x, 32 devices: a whole 2x2x4 slice. The times are simulated.
32 devices in a mesh: ctx: 16 (over z, y, x), head: 2 (over core).
Axes of the slice: x: 2, y: 2, z: 4, core: 2. Of those that a mesh axis runs over, the one named last changes fastest.
Arguments:
- inputs: bfloat16 [2048, 2048], P('ctx', 'head'), may hold values from -6 to 6
- queries: bfloat16 [2048, 32, 128], P('ctx', 'head'), may hold values from -6 to 6
- keys: bfloat16 [2048, 4, 128], P('ctx', 'head'), may hold values from -6 to 6
- values: bfloat16 [2048, 4, 128], P('ctx', 'head'), may hold values from -6 to 6
- lengths: int32 [4], replicated, may hold values from 1 to 1024, 2048 in all
- out_weight: bfloat16 [4096, 2048], P('head'), may hold values from -0.09375 to 0.09375
- norm_gain: bfloat16 [2048], P('head'), may hold values from 0.099609375 to 1.8984375
- expert_ids: int32 [2048, 8], P('ctx'), may hold values from 0 to 31, all different within a row; in each aligned block of 128 rows (0 to 127, 128 to 255, ...) at most 40 rows name the same one
- gate_codes: int32 [2048, 8], P('ctx'), may hold values from 1 to 16
- gate_weight: bfloat16 [32, 2048, 768], P('ctx', None, 'head'), may hold values from -0.125 to 0.125
- up_weight: bfloat16 [32, 2048, 768], P('ctx', None, 'head'), may hold values from -0.125 to 0.125
- down_weight: bfloat16 [32, 768, 2048], P('ctx', 'head'), may hold values from -0.4375 to 0.4375
- cotangent: bfloat16 [2048, 2048], P('ctx', 'head'), may hold values from -6 to 6
Outputs:
- output: bfloat16 [2048, 2048], P('ctx', 'head')
- input_grad: bfloat16 [2048, 2048], P('ctx', 'head')
- down_grad: bfloat16 [32, 768, 2048], P('ctx', 'head')
- norm_term: float32 [2048], P('ctx')
Inputs may be any that keep to these rules, and one draw needn't show every extreme that they name: `expert_ids`: the 128 rows of one index of ctx name one expert at most 40 times, a bound that some block reaches. The lengths sum to 2048; the largest is 1024.
All inputs are finite; a program needn't handle non-finite values.
Results may differ from a plain program's by a relative error of at most 0.023.
Values may be sent and summed in bfloat16 or wider, within the bound.
No kernel may reach another device: no remote copies, remote signals or barrier semaphores. Data moves between devices by JAX's collectives and lax.ppermute only.
A program may use at most 256 MiB of HBM per device.

v0:
```python
import jax
import jax.numpy as jnp
from jax import lax
from jax.sharding import PartitionSpec as P

D = 2048
TOP = 8
EXP_DEV = 2
TOK_DEV = 128


def stored_places(rownum, devices, per_device):
    owner = rownum // per_device
    within = rownum % per_device
    half = per_device // 2
    return jnp.where(
        within < half, owner * half + within, (2 * devices - 1 - owner) * half + within - half
    )


def document_ids(places, lengths):
    ends = jnp.cumsum(lengths)
    return jnp.sum((places[:, None] >= ends[None, :]).astype(jnp.int32), axis=1)


def local(
    inputs,
    queries,
    keys,
    values,
    lengths,
    out_weight,
    norm_gain,
    expert_ids,
    gate_codes,
    gate_weight,
    up_weight,
    down_weight,
    cotangent,
):
    devices = lax.axis_size("ctx")
    position = lax.axis_index("ctx")
    local_tokens, local_heads, head_width = queries.shape
    kv_heads = keys.shape[1]
    head_groups = local_heads // kv_heads
    scale = head_width ** (-0.5)
    query_rows = position * local_tokens + jnp.arange(local_tokens, dtype=jnp.int32)
    query_places = stored_places(query_rows, devices, local_tokens)
    query_docs = document_ids(query_places, lengths)
    grouped = queries.reshape(local_tokens, kv_heads, head_groups, head_width)
    key_piece = lax.all_gather(keys, "ctx", axis=0, tiled=True)
    value_piece = lax.all_gather(values, "ctx", axis=0, tiled=True)
    count = key_piece.shape[0]
    key_places = stored_places(jnp.arange(count, dtype=jnp.int32), devices, local_tokens)
    key_docs = document_ids(key_places, lengths)
    allowed = (key_places[None, :] <= query_places[:, None]) & (
        key_docs[None, :] == query_docs[:, None]
    )
    highest = jnp.full((local_tokens, kv_heads, head_groups), -1e30, jnp.float32)
    scores = (
        jnp.einsum("qkgd,skd->qkgs", grouped, key_piece, preferred_element_type=jnp.float32) * scale
    )
    visible = allowed[:, None, None, :]
    newest = jnp.maximum(highest, jnp.max(jnp.where(visible, scores, -1e30), axis=3))
    weights = jnp.where(visible, jnp.exp(scores - newest[..., None]), 0.0)
    denominator = jnp.sum(weights, axis=3)
    accumulated = jnp.einsum(
        "qkgs,skd->qkgd",
        weights.astype(jnp.bfloat16),
        value_piece,
        preferred_element_type=jnp.float32,
    )
    highest, denominator, accumulated = (newest, denominator, accumulated)
    heads = (
        (accumulated / denominator[..., None])
        .astype(jnp.bfloat16)
        .reshape(local_tokens, local_heads * head_width)
    )
    partial_proj = jnp.dot(heads, out_weight, preferred_element_type=jnp.float32)
    projected = lax.psum_scatter(
        partial_proj.astype(jnp.bfloat16), "head", scatter_dimension=1, tiled=True
    ).astype(jnp.float32)
    stream = (inputs.astype(jnp.float32) + projected).astype(jnp.bfloat16)
    wide = stream.astype(jnp.float32)
    squares = lax.psum(jnp.sum(wide * wide, axis=1), "head")
    inverse = lax.rsqrt(squares / D + 1e-06)[:, None]
    gain = norm_gain.astype(jnp.float32)
    normed = (wide * inverse * gain).astype(jnp.bfloat16)
    experts_all = EXP_DEV * devices
    capacity = max(2, 5 * TOK_DEV * TOP // (4 * experts_all))
    half_width = wide.shape[1]
    flat_experts = expert_ids.reshape(-1)
    onehot = (flat_experts[:, None] == jnp.arange(experts_all, dtype=jnp.int32)[None, :]).astype(
        jnp.int32
    )
    slots = jnp.sum((jnp.cumsum(onehot, axis=0) - 1) * onehot, axis=1)
    targets = flat_experts * capacity + slots
    sources = jnp.arange(flat_experts.shape[0], dtype=jnp.int32) // TOP

    def place_rows(rows):
        buffer = (
            jnp.zeros((experts_all * capacity, rows.shape[1]), rows.dtype).at[targets].set(rows)
        )
        return buffer.reshape(devices, EXP_DEV, capacity, rows.shape[1])

    arrived = lax.all_to_all(
        place_rows(normed[sources]), "ctx", split_axis=0, concat_axis=0, tiled=True
    )
    features = lax.all_gather(arrived, "head", axis=3, tiled=True)
    gate = jnp.einsum("necd,edf->necf", features, gate_weight, preferred_element_type=jnp.float32)
    upper = jnp.einsum("necd,edf->necf", features, up_weight, preferred_element_type=jnp.float32)
    activated = jax.nn.silu(gate)
    units = (activated * upper).astype(jnp.bfloat16)
    partial_out = jnp.einsum(
        "necf,efd->necd", units, down_weight, preferred_element_type=jnp.float32
    )
    summed = lax.psum(partial_out.astype(jnp.bfloat16), "head").astype(jnp.float32)
    summed = lax.dynamic_slice_in_dim(summed, lax.axis_index("head") * half_width, half_width, 3)
    returned = lax.all_to_all(
        summed.astype(jnp.bfloat16), "ctx", split_axis=0, concat_axis=0, tiled=True
    )
    picked = returned.reshape(experts_all * capacity, half_width)[targets].astype(jnp.float32)
    picked = picked.reshape(local_tokens, TOP, half_width)
    shares = gate_codes.astype(jnp.float32)
    shares = shares / jnp.sum(shares, axis=1, keepdims=True)
    mixture = jnp.sum(picked * shares[:, :, None], axis=1)
    output = (wide + mixture).astype(jnp.bfloat16)
    upstream = cotangent.astype(jnp.float32)
    routed_rows = (
        (shares[:, :, None] * upstream[:, None, :]).astype(jnp.bfloat16).reshape(-1, half_width)
    )
    incoming = lax.all_to_all(
        place_rows(routed_rows), "ctx", split_axis=0, concat_axis=0, tiled=True
    )
    incoming = lax.all_gather(incoming, "head", axis=3, tiled=True)
    units_grad = jnp.einsum(
        "necd,efd->necf", incoming, down_weight, preferred_element_type=jnp.float32
    )
    sigmoid_gate = jax.nn.sigmoid(gate)
    gate_grad = (units_grad * upper * sigmoid_gate * (1.0 + gate * (1.0 - sigmoid_gate))).astype(
        jnp.bfloat16
    )
    up_grad = (units_grad * activated).astype(jnp.bfloat16)
    down_grad = jnp.einsum(
        "necf,necd->efd", units, incoming, preferred_element_type=jnp.float32
    ).astype(jnp.bfloat16)
    input_part = jnp.einsum(
        "necf,edf->necd", gate_grad, gate_weight, preferred_element_type=jnp.float32
    ) + jnp.einsum("necf,edf->necd", up_grad, up_weight, preferred_element_type=jnp.float32)
    input_share = lax.psum_scatter(
        input_part.astype(jnp.bfloat16), "head", scatter_dimension=3, tiled=True
    )
    backward_rows = lax.all_to_all(input_share, "ctx", split_axis=0, concat_axis=0, tiled=True)
    gathered = backward_rows.reshape(experts_all * capacity, half_width)[targets].astype(
        jnp.float32
    )
    gathered = gathered.reshape(local_tokens, TOP, half_width)
    scaled = jnp.sum(gathered, axis=1) * gain
    inner = lax.psum(jnp.sum(scaled * wide, axis=1), "head")[:, None]
    input_grad = (upstream + inverse * scaled - wide * inverse**3 * inner / D).astype(jnp.bfloat16)
    norm_term = (inverse**2 * inner / D**0.5)[:, 0]
    return (output, input_grad, down_grad, norm_term)


def solution(mesh):
    in_specs = (
        P("ctx", "head"),
        P("ctx", "head", None),
        P("ctx", "head", None),
        P("ctx", "head", None),
        P(),
        P("head", None),
        P("head"),
        P("ctx", None),
        P("ctx", None),
        P("ctx", None, "head"),
        P("ctx", None, "head"),
        P("ctx", "head", None),
        P("ctx", "head"),
    )
    out_specs = (P("ctx", "head"), P("ctx", "head"), P("ctx", "head", None), P("ctx"))
    return jax.shard_map(local, mesh=mesh, in_specs=in_specs, out_specs=out_specs, check_vma=False)
```

profile of v0, /device:TPU:13, one launch (start us, length us, event | category | flops | bytes accessed | tf_op | source)
XLA Modules:
  0.0 517.6 jit_solution(15707918158378483061)
XLA Ops:
  7.2 1.6 copy.52
  8.9 1.6 copy.54
  10.6 0.8 copy.57
  11.4 0.1 eq.53
  11.5 0.1 eq.49
  11.6 0.8 reduce-window.18
  12.4 0.6 convert_reduce_fusion.3
  13.0 0.7 convert_reduce_fusion.1
  13.7 0.7 convert_element_type.108
  14.4 9.0 %reduce-window.19 = s32[32,8,128]{2,1,0:T(8,128)S(1)} reduce-window(s32[32,8,128]{2,1,0:T(8,128)S(1)} %fusion.63, s32[]{:T(128)} %constant.106.clone.1), window={size=1x1x128 pad=0_0x0_0x127_0}, to_apply=%region_6.7 | reduce-window | flops 4161536 | bytes 262148 | tf_op jit(solution)/shard_map/reduce-window.1
  23.5 0.1 copy.59
  23.7 0.7 copy.60
  24.4 2.6 compare_and_fusion
  27.0 38.7 %all-gather.5.cloned.1.call-done = bf16[2048,2,128]{2,0,1:T(8,128)(2,1)} async-done(((bf16[128,2,128]{2,0,1:T(8,128)(2,1)}), bf16[2048,2,128]{2,0,1:T(8,128)(2,1)}) %all-gather.5.cloned.1.call-update) | async-done | bytes 1048592 | tf_op jit(solution)/shard_map/all_gather | solution.py:51
  65.7 9.5 %fusion = (f32[128,2,8]{0,2,1:T(8,128)S(1)}, f32[2,2048,128,8]{2,1,3,0:T(8,128)}) fusion(pred[128,2048]{0,1:T(8,128)(4,1)S(1)} %compare_and_fusion, bf16[128,2,8,128]{3,2,1,0:T(8,128)(2,1)} %bitcast.157, bf16[2048,2,128]{2,0,1:T(8,128)(2,1)} %all-gather.5.cloned.1.call-done), kind=kOutput, calls=%fused_computation.7 | convolution fusion | flops 1086322688 | bytes 18620416 | tf_op jit(solution)/shard_map/qkgd,skd->qkgs/dot_general | solution.py:61
  75.2 9.8 %fusion.3 = f32[128,2,8]{0,2,1:T(8,128)} fusion(f32[2,2048,128,8]{2,1,3,0:T(8,128)} %get-tuple-element.11, f32[128,2,8]{0,2,1:T(8,128)S(1)} %broadcast_maximum_fusion, pred[128,2048]{0,1:T(8,128)(4,1)S(1)} %compare_and_fusion), kind=kLoop, calls=%fused_computation.10 | loop fusion | flops 16775168 | bytes 17055744 | tf_op jit(solution)/shard_map/reduce_sum | solution.py:66
  85.0 34.8 %all-gather.7.cloned.1.call-done = bf16[2048,2,128]{0,2,1:T(8,128)(2,1)} async-done(((bf16[128,2,128]{0,2,1:T(8,128)(2,1)}), bf16[2048,2,128]{0,2,1:T(8,128)(2,1)}) %all-gather.7.cloned.1.call-update) | async-done | bytes 1048592 | tf_op jit(solution)/shard_map/all_gather | solution.py:52
  119.8 9.2 %divide_convert_fusion = bf16[128,2,8,128]{0,3,2,1:T(8,128)(2,1)S(1)} fusion(f32[2,2048,128,8]{2,1,3,0:T(8,128)} %get-tuple-element.11, f32[128,2,8]{0,2,1:T(8,128)S(1)} %broadcast_maximum_fusion, pred[128,2048]{0,1:T(8,128)(4,1)S(1)} %compare_and_fusion, bf16[2048,2,128]{0,2,1:T(8,128)(2,1)} %all-gather.7.cloned.1.call-done, f32[128,2,8]{0,2,1:T(8,128)} %fusion.3), kind=kOutput, calls=%fused_computation.66 | convolution fusion | flops 1091043328 | bytes 18628608 | tf_op jit(solution)/shard_map/qkgs,skd->qkgd/dot_general | solution.py:67
  129.1 5.5 %convolution_convert_fusion = bf16[128,2048]{1,0:T(8,128)(2,1)} fusion(bf16[128,2048]{0,1:T(8,128)(2,1)S(1)} %bitcast.156, bf16[2048,2048]{1,0:T(8,128)(2,1)} %param.18), kind=kOutput, calls=%fused_computation.34 | convolution fusion | flops 1074003968 | bytes 9437184 | tf_op jit(solution)/shard_map/dot_general | solution.py:79
  134.6 0.2 all-gather.9.cloned.1.call-start
  134.8 0.1 copy.56
  134.9 0.1 mul.186
  135.0 0.1 add_add_fusion
  135.2 9.1 %reduce-scatter.3.cloned.1.call-done = bf16[128,1024]{1,0:T(8,128)(2,1)} async-done(((bf16[128,2048]{1,0:T(8,128)(2,1)}), bf16[128,1024]{1,0:T(8,128)(2,1)}) %reduce-scatter.3.cloned.1.call-update) | async-done | bytes 262160 | tf_op jit(solution)/shard_map/reduce_scatter | solution.py:80
  144.3 1.2 fusion.51
  145.5 2.5 psum.21
  147.9 0.8 fusion.53
  148.8 16.4 %scatter_custom_fusion = bf16[1280,1024]{1,0:T(8,128)(2,1)} fusion(s32[1024]{0:T(1024)S(1)} %bitcast.161, bf16[128,1024]{1,0:T(8,128)(2,1)} %fusion.53, s32[1024]{0:T(1024)S(1)} %broadcast_clamp_fusion.1, bf16[]{:T(256)} %constant.120.clone.1), kind=kCustom, calls=%fused_computation.36 | custom fusion | bytes 2621952 | tf_op jit(solution)/shard_map/scatter | solution.py:102
  165.2 64.9 %all_to_all.20 = bf16[16,2,40,1024]{3,2,1,0:T(8,128)(2,1)S(1)} all-to-all(bf16[16,2,40,1024]{3,2,1,0:T(8,128)(2,1)} %bitcast.155), channel_id=1, replica_groups=mesh['ctx'=16,'head'=2] {'ctx'}, dimensions={0} | all-to-all | bytes 5242880 | tf_op jit(solution)/shard_map/all_to_all | solution.py:106
  230.1 1.8 copy.61
  231.9 0.6 copy-done.9
  232.5 0.1 copy.63
  232.6 0.1 mul.198
  232.7 1.8 convert_element_type.119
  234.6 8.0 %scatter_custom_fusion.1 = bf16[1280,1024]{1,0:T(8,128)(2,1)} fusion(s32[1024]{0:T(1024)S(1)} %bitcast.162, f32[128,1024]{1,0:T(8,128)} %convert_element_type.119, f32[1024]{0:T(1024)S(1)} %mul.198, bf16[]{:T(256)} %constant.120.clone.1), kind=kCustom, calls=%fused_computation.35 | custom fusion | flops 2097152 | bytes 3149826 | tf_op jit(solution)/shard_map/scatter | solution.py:102
  242.5 63.1 %all_to_all.21 = bf16[16,2,40,1024]{3,2,1,0:T(8,128)(2,1)S(1)} all-to-all(bf16[16,2,40,1024]{3,2,1,0:T(8,128)(2,1)} %bitcast.154), channel_id=1, replica_groups=mesh['ctx'=16,'head'=2] {'ctx'}, dimensions={0} | all-to-all | bytes 5242880 | tf_op jit(solution)/shard_map/all_to_all | solution.py:132
  305.7 1.7 copy.65
  307.5 5.9 %fusion.16 = f32[2,16,40,384]{3,2,1,0:T(8,128)S(1)} fusion(bf16[16,2,40,2048]{3,2,0,1:T(8,128)(2,1)} %all-gather.9.cloned.1.call-done, bf16[2,2048,384]{2,1,0:T(8,128)(2,1)} %param.22), kind=kOutput, calls=%fused_computation.29 | convolution fusion | flops 2013265920 | bytes 10354688 | tf_op jit(solution)/shard_map/necd,edf->necf/dot_general | solution.py:110
  313.5 4.3 fusion.31
  317.8 0.9 copy-done.13
  318.7 4.6 convert_bitcast_fusion
  323.5 0.4 all-gather.11.cloned.1.call-done
  323.8 5.9 %fusion.18 = f32[2,16,40,384]{3,2,1,0:T(8,128)S(1)} fusion(bf16[16,2,40,2048]{3,2,0,1:T(8,128)(2,1)} %all-gather.11.cloned.1.call-done, bf16[2,384,2048]{2,1,0:T(8,128)(2,1)} %param.24), kind=kOutput, calls=%fused_computation.31 | convolution fusion | flops 2013265920 | bytes 10354688 | tf_op jit(solution)/shard_map/necd,efd->necf/dot_general | solution.py:136
  329.8 6.6 %fusion.14 = f32[2,16,40,2048]{3,2,1,0:T(8,128)} fusion(bf16[2,2048,384]{2,1,0:T(8,128)(2,1)S(1)} %copy-done.5, f32[2,16,40,384]{3,2,1,0:T(8,128)S(1)} %fusion.18, f32[2,16,40,384]{3,2,1,0:T(8,128)S(1)} %copy-done.6, f32[2,16,40,384]{3,2,1,0:T(8,128)S(1)} %copy-done.3), kind=kOutput, calls=%fused_computation.27 | convolution fusion | flops 2018181120 | bytes 19529728 | tf_op jit(solution)/shard_map/necf,edf->necd/dot_general | solution.py:147
  336.4 8.3 %fusion.8 = bf16[16,2,40,2048]{3,2,0,1:T(8,128)(2,1)} fusion(f32[2,16,40,2048]{3,2,1,0:T(8,128)} %fusion.14, bf16[2,2048,384]{2,1,0:T(8,128)(2,1)S(1)} %copy-done, f32[2,16,40,384]{3,2,1,0:T(8,128)S(1)} %fusion.18, f32[2,16,40,384]{3,2,1,0:T(8,128)S(1)} %copy-done.3), kind=kOutput, calls=%fused_computation.16 | convolution fusion | flops 2021457920 | bytes 22806528 | tf_op jit(solution)/shard_map/necf,edf->necd/dot_general | solution.py:149
  344.7 13.0 %all-reduce.2.cloned.1.call-done = bf16[16,2,40,2048]{3,2,0,1:T(8,128)(2,1)} async-done(((bf16[16,2,40,2048]{3,2,0,1:T(8,128)(2,1)}), bf16[16,2,40,2048]{3,2,0,1:T(8,128)(2,1)}) %all-reduce.2.cloned.1.call-update) | async-done | bytes 5242896 | tf_op jit(solution)/shard_map/psum | solution.py:117
  357.7 2.0 convert_convert_fusion
  359.7 1.8 copy.62
  361.5 6.4 %all-to-all-start.1 = ((bf16[16,2,40,1024]{3,2,1,0:T(8,128)(2,1)}), bf16[16,2,40,1024]{3,2,1,0:T(8,128)(2,1)S(1)}, u32[]{:S(2)}, u32[]{:S(2)}) async-start(bf16[16,2,40,1024]{3,2,1,0:T(8,128)(2,1)} %copy.62), calls=%async_computation.2 | async-start | bytes 5242880 | tf_op jit(solution)/shard_map/all_to_all | solution.py:119
  367.9 6.5 %reduce-scatter.5.cloned.1.call-done = bf16[16,2,40,1024]{3,2,0,1:T(8,128)(2,1)} async-done(((bf16[16,2,40,2048]{3,2,0,1:T(8,128)(2,1)}), bf16[16,2,40,1024]{3,2,0,1:T(8,128)(2,1)}) %reduce-scatter.5.cloned.1.call-update) | async-done | bytes 2621456 | tf_op jit(solution)/shard_map/reduce_scatter | solution.py:150
  374.4 3.6 copy.66
  378.0 49.0 %all-to-all-done.1 = bf16[16,2,40,1024]{3,2,1,0:T(8,128)(2,1)S(1)} async-done(((bf16[16,2,40,1024]{3,2,1,0:T(8,128)(2,1)}), bf16[16,2,40,1024]{3,2,1,0:T(8,128)(2,1)S(1)}, u32[]{:S(2)}, u32[]{:S(2)}) %all-to-all-start.1) | async-done | bytes 2621472 | tf_op jit(solution)/shard_map/all_to_all | solution.py:119
  427.0 5.5 %all-to-all-start.3 = ((bf16[16,2,40,1024]{3,2,1,0:T(8,128)(2,1)}), bf16[16,2,40,1024]{3,2,1,0:T(8,128)(2,1)}, u32[]{:S(2)}, u32[]{:S(2)}) async-start(bf16[16,2,40,1024]{3,2,1,0:T(8,128)(2,1)} %copy.66), calls=%async_computation.5 | async-start | bytes 5242880 | tf_op jit(solution)/shard_map/all_to_all | solution.py:153
  432.6 7.1 %bitcast_convert_fusion = bf16[2,384,2048]{2,1,0:T(8,128)(2,1)} fusion(bf16[16,2,40,384]{3,2,0,1:T(8,128)(2,1)} %copy-done.13, bf16[16,2,40,2048]{3,2,0,1:T(8,128)(2,1)} %all-gather.11.cloned.1.call-done), kind=kOutput, calls=%fused_computation.15 | convolution fusion | flops 2014838784 | bytes 9371648 | tf_op jit(solution)/shard_map/necf,necd->efd/dot_general | solution.py:144
  439.7 5.4 %gather_fusion = bf16[1024,1024]{1,0:T(8,128)(2,1)} fusion(bf16[1280,1024]{1,0:T(8,128)(2,1)S(1)} %bitcast.153, s32[1024]{0:T(1024)S(1)} %broadcast_clamp_fusion), kind=kCustom, calls=%fused_computation.1 | custom fusion | bytes 4198400 | tf_op jit(solution)/shard_map/gather | solution.py:122
  445.0 3.7 fusion.9
  448.8 42.9 %all-to-all-done.3 = bf16[16,2,40,1024]{3,2,1,0:T(8,128)(2,1)} async-done(((bf16[16,2,40,1024]{3,2,1,0:T(8,128)(2,1)}), bf16[16,2,40,1024]{3,2,1,0:T(8,128)(2,1)}, u32[]{:S(2)}, u32[]{:S(2)}) %all-to-all-start.3) | async-done | bytes 2621472 | tf_op jit(solution)/shard_map/all_to_all | solution.py:153
  491.6 8.3 %gather_fusion.1 = bf16[1024,1024]{1,0:T(8,128)(2,1)} fusion(bf16[1280,1024]{1,0:T(8,128)(2,1)} %bitcast.34, s32[1024]{0:T(1024)S(1)} %broadcast_clamp_fusion), kind=kCustom, calls=%fused_computation.2 | custom fusion | bytes 4198400 | tf_op jit(solution)/shard_map/gather | solution.py:154
  499.9 3.0 convert_reduce_fusion
  502.9 0.8 copy-done.4
  503.7 0.2 fusion.59
  503.9 3.6 psum.23
  507.4 0.5 fusion.79
  508.0 2.3 fusion.58
  (55 shorter events, 0.7 us)
Async XLA Ops:
  7.2 306.3 %copy-start = (bf16[2,2048,384]{2,1,0:T(8,128)(2,1)S(1)}, bf16[2,2048,384]{2,1,0:T(8,128)(2,1)}, u32[]{:S(2)}) copy-start(bf16[2,2048,384]{2,1,0:T(8,128)(2,1)} %param.23) | copy-start | bytes 9437188
  7.2 58.5 %all-gather.5.cloned.1.call-start = ((), (), s32[]{:S(2)}) async-start(), calls=%async_computation.6 | async-start | bytes 1114112 | tf_op jit(solution)/shard_map/all_gather | solution.py:51
  8.9 110.9 %all-gather.7.cloned.1.call-start = ((), (), s32[]{:S(2)}) async-start(), calls=%async_computation.7 | async-start | bytes 1114112 | tf_op jit(solution)/shard_map/all_gather | solution.py:52
  10.5 133.7 %reduce-scatter.3.cloned.1.call-start = ((), (), s32[]{:S(2)}) async-start(), calls=%async_computation.8 | async-start | bytes 786432 | tf_op jit(solution)/shard_map/reduce_scatter | solution.py:80
  11.6 1.4 copy-start.10
  129.0 5.7 %copy-start.8 = (s32[128,8]{0,1:T(8,128)S(1)}, s32[128,8]{0,1:T(8,128)}, u32[]{:S(2)}) copy-start(s32[128,8]{0,1:T(8,128)} %param.20) | copy-start | bytes 12292
  129.0 6.0 %copy-start.7 = (s32[32,8]{1,0:T(8,128)S(1)}, s32[32,8]{1,0:T(8,128)}, u32[]{:S(2)}) copy-start(s32[32,8]{1,0:T(8,128)} %copy.60) | copy-start | bytes 3076
  134.6 173.0 %all-gather.9.cloned.1.call-start = ((), (), s32[]{:S(2)}) async-start(), calls=%async_computation.9 | async-start | bytes 7864320 | tf_op jit(solution)/shard_map/all_gather | solution.py:109
  231.8 0.7 copy-start.9
  231.9 92.0 %all-gather.11.cloned.1.call-start = ((), (), s32[]{:S(2)}) async-start(), calls=%async_computation.11 | async-start | bytes 7864320 | tf_op jit(solution)/shard_map/all_gather | solution.py:135
  307.4 50.2 %all-reduce.2.cloned.1.call-start = ((), (), s32[]{:S(2)}) async-start(), calls=%async_computation.10 | async-start | bytes 10485760 | tf_op jit(solution)/shard_map/psum | solution.py:117
  307.5 6.0 %copy-start.11 = (bf16[16,2,40,2048]{3,2,0,1:T(8,128)(2,1)S(1)}, bf16[16,2,40,2048]{3,2,0,1:T(8,128)(2,1)}, u32[]{:S(2)}) copy-start(bf16[16,2,40,2048]{3,2,0,1:T(8,128)(2,1)} %all-gather.9.cloned.1.call-done) | copy-start | bytes 15728644
  313.5 4.3 copy-start.2
  313.5 5.2 %copy-start.12 = (bf16[2,384,2048]{2,1,0:T(8,128)(2,1)S(1)}, bf16[2,384,2048]{2,1,0:T(8,128)(2,1)}, u32[]{:S(2)}) copy-start(bf16[2,384,2048]{2,1,0:T(8,128)(2,1)} %param.24) | copy-start | bytes 9437188
  317.8 0.9 copy-start.13
  323.4 51.0 %reduce-scatter.5.cloned.1.call-start = ((), (), s32[]{:S(2)}) async-start(), calls=%async_computation.12 | async-start | bytes 7864320 | tf_op jit(solution)/shard_map/reduce_scatter | solution.py:150
  323.8 5.9 %copy-start.3 = (f32[2,16,40,384]{3,2,1,0:T(8,128)S(1)}, f32[2,16,40,384]{3,2,1,0:T(8,128)}, u32[]{:S(2)}) copy-start(f32[2,16,40,384]{3,2,1,0:T(8,128)} %copy-done.2) | copy-start | bytes 5898244
  323.8 5.9 %copy-start.5 = (bf16[2,2048,384]{2,1,0:T(8,128)(2,1)S(1)}, bf16[2,2048,384]{2,1,0:T(8,128)(2,1)}, u32[]{:S(2)}) copy-start(bf16[2,2048,384]{2,1,0:T(8,128)(2,1)} %param.22) | copy-start | bytes 9437188
  323.8 5.9 %copy-start.6 = (f32[2,16,40,384]{3,2,1,0:T(8,128)S(1)}, f32[2,16,40,384]{3,2,1,0:T(8,128)}, u32[]{:S(2)}) copy-start(f32[2,16,40,384]{3,2,1,0:T(8,128)} %get-tuple-element.13) | copy-start | bytes 5898244
  361.5 65.5 %all-to-all-start.1 = ((bf16[16,2,40,1024]{3,2,1,0:T(8,128)(2,1)}), bf16[16,2,40,1024]{3,2,1,0:T(8,128)(2,1)S(1)}, u32[]{:S(2)}, u32[]{:S(2)}) async-start(bf16[16,2,40,1024]{3,2,1,0:T(8,128)(2,1)} %copy.62), calls=%async_computation.2 | async-start | bytes 5242880 | tf_op jit(solution)/shard_map/all_to_all | solution.py:119
  427.0 64.6 %all-to-all-start.3 = ((bf16[16,2,40,1024]{3,2,1,0:T(8,128)(2,1)}), bf16[16,2,40,1024]{3,2,1,0:T(8,128)(2,1)}, u32[]{:S(2)}, u32[]{:S(2)}) async-start(bf16[16,2,40,1024]{3,2,1,0:T(8,128)(2,1)} %copy.66), calls=%async_computation.5 | async-start | bytes 5242880 | tf_op jit(solution)/shard_map/all_to_all | solution.py:153
  491.6 18.7 %copy-start.1 = (bf16[2,2048,384]{2,1,0:T(8,128)(2,1)S(1)}, bf16[2,2048,384]{2,1,0:T(8,128)(2,1)}, u32[]{:S(2)}) copy-start(bf16[2,2048,384]{2,1,0:T(8,128)(2,1)} %param.23) | copy-start | bytes 9437188
  502.9 0.8 copy-start.4
Sparse Core Ops, SparseCore 0:
  11.3 54.2 all-gather.4
  69.0 50.8 all-gather.6
  134.7 9.5 reduce-scatter.2
  232.0 15.9 all-gather.8
  307.6 16.1 all-gather.10
  326.3 31.2 all-reduce.1
  360.0 14.3 reduce-scatter.4
where the time goes:
time: 527 us; the launch traced here: 518 us
  waiting for transfers between devices  194 us (37%)
  blocking collectives  134 us (25%)
  matrix products  67 us (13%)
  other arithmetic  48 us (9%)
  local copies, waits for them, and re-layouts  46.9 us (9%)
  between operations  14.9 us (3%)
  starting transfers between devices  12.4 us (2%)
    all_to_all x1, blocking collectives, local(): lax.all_to_all(place_rows(normed[sources]), 'ctx', split_axis=0, concat_a...  64.9 us
    all_to_all x1, blocking collectives, local(): lax.all_to_all(place_rows(routed_rows), 'ctx', split_axis=0, concat_axis=...  63.1 us
    all_to_all x1, waiting for transfers between devices, local(): lax.all_to_all(summed.astype(jnp.bfloat16), 'ctx', split_axis=0, concat_a...  49 us
    all_to_all x1, waiting for transfers between devices, local(): lax.all_to_all(input_share, 'ctx', split_axis=0, concat_axis=0, tiled=True)  42.9 us
    all_gather x1, waiting for transfers between devices, local(): key_piece = lax.all_gather(keys, 'ctx', axis=0, tiled=True)  38.7 us
    all_gather x1, waiting for transfers between devices, local(): value_piece = lax.all_gather(values, 'ctx', axis=0, tiled=True)  34.8 us
    scatter x1, local copies, waits for them, and re-layouts, place_rows(): jnp.zeros((experts_all * capacity, rows.shape[1]), rows.dtype).at[targets]  16.4 us
    psum x1, waiting for transfers between devices, local(): lax.psum(partial_out.astype(jnp.bfloat16), 'head').astype(jnp.float32)  13 us
  transfers between devices with their start and end apart: 9, of which 8 were waited for; matrix products, arithmetic and copies ran while one was open for 21% of the time, Pallas kernels for 0%

commit v1 on v0

v1 whole, which is shorter than its diff:
```python
import jax
import jax.numpy as jnp
from jax import lax
from jax.sharding import PartitionSpec as P

D = 2048
TOP = 8
EXP_DEV = 2
TOK_DEV = 128
BF = jnp.bfloat16
F32 = jnp.float32
AXES = ("ctx", "head")


def grid_of(devices):
    side = 2 if devices < 64 else 4
    return devices // (side * side), side


def exchange(array, devices, masks):
    pairs = [
        (c * 2 + h, (c ^ masks[h]) * 2 + h) for c in range(devices) for h in range(2)
    ]
    return lax.ppermute(array, AXES, pairs)


def swap_cores(array, devices):
    pairs = [(c * 2 + h, c * 2 + 1 - h) for c in range(devices) for h in range(2)]
    return lax.ppermute(array, AXES, pairs)


def local(
    inputs,
    queries,
    keys,
    values,
    lengths,
    out_weight,
    norm_gain,
    expert_ids,
    gate_codes,
    gate_weight,
    up_weight,
    down_weight,
    cotangent,
):
    devices = lax.axis_size("ctx")
    position = lax.axis_index("ctx")
    head = lax.axis_index("head")
    deep, side = grid_of(devices)
    plane = side * side

    def z_masks(k):
        return (k * plane, k * plane)

    def a_masks(k):
        return (k, k * side)

    def b_masks(k):
        return (k * side, k)

    def along(array, masks_of, count):
        return [array] + [exchange(array, devices, masks_of(k)) for k in range(1, count)]

    local_tokens, local_heads, head_width = queries.shape
    kv_heads = keys.shape[1]
    head_groups = local_heads // kv_heads
    half_width = inputs.shape[1]
    capacity = max(2, 5 * TOK_DEV * TOP // (4 * EXP_DEV * devices))
    block_rows = -(-deep * capacity // 16) * 16

    packed = jnp.concatenate(
        [
            keys.transpose(1, 0, 2).reshape(kv_heads * local_tokens, head_width),
            values.transpose(1, 0, 2).reshape(kv_heads * local_tokens, head_width),
            expert_ids.T.astype(BF),
            gate_codes.T.astype(BF),
        ],
        axis=0,
    )
    pack_z = jnp.stack(along(packed, z_masks, deep))
    pack_a = jnp.stack(along(pack_z, a_masks, side))
    pack_b = jnp.stack(along(pack_a, b_masks, side))
    chunks = devices
    pack_all = pack_b.reshape(chunks, packed.shape[0], head_width)
    key_piece = pack_all[:, : kv_heads * local_tokens].reshape(
        chunks, kv_heads, local_tokens, head_width
    )
    value_piece = pack_all[:, kv_heads * local_tokens : 2 * kv_heads * local_tokens].reshape(
        chunks, kv_heads, local_tokens, head_width
    )

    order = jnp.arange(chunks, dtype=jnp.int32)
    z_part, a_part, b_part = order % deep, order // deep % side, order // (deep * side)
    shift = jnp.where(head == 0, a_part + b_part * side, a_part * side + b_part)
    sources = position ^ (z_part * plane + shift)

    def places_of(owner):
        within = jnp.arange(local_tokens, dtype=jnp.int32)
        half = local_tokens // 2
        owner = owner[..., None]
        return jnp.where(
            within < half, owner * half + within, (2 * devices - 1 - owner) * half + within - half
        )

    docs_in = lengths.shape[0]
    upto = jnp.arange(docs_in)[:, None] <= jnp.arange(docs_in)[None, :]
    ends = jnp.sum(jnp.where(upto, lengths[:, None], 0), axis=0)

    def docs_of(places):
        return jnp.sum((places[..., None] >= ends).astype(jnp.int32), axis=-1)

    query_places = places_of(position[None])[0]
    query_docs = docs_of(query_places)
    key_places = places_of(sources)
    key_docs = docs_of(key_places)
    allowed = (key_places[None] <= query_places[:, None, None]) & (
        key_docs[None] == query_docs[:, None, None]
    )
    scale = head_width ** (-0.5)
    grouped = queries.reshape(local_tokens, kv_heads, head_groups, head_width).transpose(1, 2, 0, 3)
    scores = jnp.einsum("kgqd,cksd->kgqcs".replace(" ", ""), grouped, key_piece, preferred_element_type=F32)
    scores = scores * scale
    masked = jnp.where(allowed, scores, -1e30)
    top = jnp.max(masked, axis=(3, 4), keepdims=True)
    weights = jnp.where(allowed, jnp.exp(scores - top), 0.0)
    denominator = jnp.sum(weights, axis=(3, 4))
    mixed = jnp.einsum("kgqcs,cksd->kgqd", weights.astype(BF), value_piece, preferred_element_type=F32)
    heads = (mixed / denominator[..., None]).astype(BF)
    heads = heads.transpose(2, 0, 1, 3).reshape(local_tokens, local_heads * head_width)

    partial_proj = jnp.dot(heads, out_weight, preferred_element_type=F32)
    mine = lax.dynamic_slice_in_dim(partial_proj, head * half_width, half_width, 1)
    theirs = lax.dynamic_slice_in_dim(partial_proj, (1 - head) * half_width, half_width, 1)
    projected = mine + swap_cores(theirs.astype(BF), devices).astype(F32)
    stream = (inputs.astype(F32) + projected).astype(BF)
    wide = stream.astype(F32)
    squares = lax.psum(jnp.sum(wide * wide, axis=1), "head")
    inverse = lax.rsqrt(squares / D + 1e-06)[:, None]
    gain = norm_gain.astype(F32)
    normed = (wide * inverse * gain).astype(BF)

    near = pack_a[..., -2 * TOP :, :].astype(jnp.int32)
    near_ids, near_codes = near[..., :TOP, :], near[..., TOP:, :].astype(F32)
    near_total = jnp.sum(near_codes, axis=-2)
    owners = position ^ (jnp.arange(side, dtype=jnp.int32) * jnp.where(head == 0, side, 1))
    experts = owners[:, None] * EXP_DEV + jnp.arange(EXP_DEV, dtype=jnp.int32)
    hit = near_ids == experts[:, :, None, None, None, None]
    share = jnp.sum(jnp.where(hit, near_codes, 0.0), axis=-2) / near_total
    member = jnp.any(hit, axis=-2)
    before = jnp.arange(local_tokens)[:, None] < jnp.arange(local_tokens)[None, :]
    rank = jnp.einsum(
        "keazt,tu->keazu", member.astype(BF), before.astype(BF), preferred_element_type=F32
    ).astype(jnp.int32)
    slot = jnp.arange(deep, dtype=jnp.int32)[:, None] * capacity + rank
    slot = jnp.where(member, slot, -1)
    tokens = deep * local_tokens
    slot = slot.reshape(side, EXP_DEV, side, tokens)
    share = share.reshape(side, EXP_DEV, side, tokens)
    hot = slot[..., None, :] == jnp.arange(block_rows, dtype=jnp.int32)[:, None]
    hot_bf = hot.astype(BF)
    slot_share = jnp.sum(jnp.where(hot, share[..., None, :], 0.0), axis=-1)

    def send_rows(rows, scaled):
        level = jnp.stack(along(rows, z_masks, deep))
        level = jnp.stack(along(level, a_masks, side)).reshape(side, tokens, half_width)
        out = jnp.einsum("kearu,aud->keard", hot_bf, level, preferred_element_type=F32)
        if scaled:
            out = out * slot_share[..., None]
        out = out.astype(BF)
        got = [out[0]] + [exchange(out[k], devices, b_masks(k)) for k in range(1, side)]
        got = jnp.stack(got)
        other = swap_cores(got, devices).transpose(2, 1, 0, 3, 4)
        return jnp.where(
            head == 0,
            jnp.concatenate([got, other], axis=-1),
            jnp.concatenate([other, got], axis=-1),
        )

    def return_rows(part, weighted):
        mine = lax.dynamic_slice_in_dim(part, head * half_width, half_width, 4)
        theirs = lax.dynamic_slice_in_dim(part, (1 - head) * half_width, half_width, 4)
        theirs = theirs.astype(BF).transpose(2, 1, 0, 3, 4)
        total = (mine + swap_cores(theirs, devices).astype(F32)).astype(BF)
        got = [total[0]] + [exchange(total[k], devices, b_masks(k)) for k in range(1, side)]
        got = jnp.stack(got)
        if weighted:
            each = jnp.einsum("kearu,keard->keaud", hot_bf, got, preferred_element_type=F32)
            dense = jnp.sum(each * share[..., None], axis=(0, 1))
        else:
            dense = jnp.einsum("kearu,keard->aud", hot_bf, got, preferred_element_type=F32)
        near_sum = dense[0]
        for k in range(1, side):
            near_sum = near_sum + exchange(dense[k].astype(BF), devices, a_masks(k)).astype(F32)
        near_sum = near_sum.reshape(deep, local_tokens, half_width)
        result = near_sum[0]
        for k in range(1, deep):
            result = result + exchange(near_sum[k].astype(BF), devices, z_masks(k)).astype(F32)
        return result

    upstream = cotangent.astype(F32)
    incoming = send_rows(cotangent, True)
    features = send_rows(normed, False)
    gate = jnp.einsum("beard,edf->bearf", features, gate_weight, preferred_element_type=F32)
    upper = jnp.einsum("beard,edf->bearf", features, up_weight, preferred_element_type=F32)
    sigmoid_gate = jax.nn.sigmoid(gate)
    activated = gate * sigmoid_gate
    units = (activated * upper).astype(BF)
    partial_out = jnp.einsum("bearf,efd->beard", units, down_weight, preferred_element_type=F32)
    mixture = return_rows(partial_out, True)
    output = (wide + mixture).astype(BF)

    units_grad = jnp.einsum("beard,efd->bearf", incoming, down_weight, preferred_element_type=F32)
    gate_grad = (units_grad * upper * sigmoid_gate * (1.0 + gate * (1.0 - sigmoid_gate))).astype(BF)
    up_grad = (units_grad * activated).astype(BF)
    down_grad = jnp.einsum(
        "bearf,beard->efd", units, incoming, preferred_element_type=F32
    ).astype(BF)
    input_part = jnp.einsum(
        "bearf,edf->beard", gate_grad, gate_weight, preferred_element_type=F32
    ) + jnp.einsum("bearf,edf->beard", up_grad, up_weight, preferred_element_type=F32)
    scaled = return_rows(input_part, False) * gain
    inner = lax.psum(jnp.sum(scaled * wide, axis=1), "head")[:, None]
    input_grad = (upstream + inverse * scaled - wide * inverse**3 * inner / D).astype(BF)
    norm_term = (inverse**2 * inner / D**0.5)[:, 0]
    return (output, input_grad, down_grad, norm_term)


def solution(mesh):
    in_specs = (
        P("ctx", "head"),
        P("ctx", "head", None),
        P("ctx", "head", None),
        P("ctx", "head", None),
        P(),
        P("head", None),
        P("head"),
        P("ctx", None),
        P("ctx", None),
        P("ctx", None, "head"),
        P("ctx", None, "head"),
        P("ctx", "head", None),
        P("ctx", "head"),
    )
    out_specs = (P("ctx", "head"), P("ctx", "head"), P("ctx", "head", None), P("ctx"))
    return jax.shard_map(local, mesh=mesh, in_specs=in_specs, out_specs=out_specs, check_vma=False)
```

time: 527 us -> 318 us (0.60)
  the two profiles are of different devices: /device:TPU:13 before, /device:TPU:0 now
where the time goes in v1:
time: 318 us; the launch traced here: 312 us
  waiting for transfers between devices  130 us (41%)
  matrix products  62.6 us (20%)
  other arithmetic  49.4 us (16%)
  starting transfers between devices  47.9 us (15%)
  local copies, waits for them, and re-layouts  15.5 us (5%)
  blocking collectives  4.93 us (2%)
    ppermute x25, waiting for transfers between devices, exchange(): return lax.ppermute(array, AXES, pairs)  130 us
    ppermute x25, starting transfers between devices, exchange(): return lax.ppermute(array, AXES, pairs)  46.6 us
    dot_general x1, matrix products, local(): jnp.einsum('kgqcs,cksd->kgqd', weights.astype(BF), value_piece, preferred...  10 us
    reduce_sum x1, other arithmetic, local(): denominator = jnp.sum(weights, axis=(3, 4))  9.1 us
    dot_general x1, matrix products, local(): jnp.einsum('kgqd,cksd->kgqcs'.replace(' ', ''), grouped, key_piece, prefe...  7.22 us
    select_n x2, other arithmetic, send_rows(): jnp.where(head == 0, jnp.concatenate([got, other], axis=-1), jnp.concaten...  6.57 us
  transfers between devices with their start and end apart: 30, of which 13 were waited for; matrix products, arithmetic and copies ran while one was open for 20% of the time, Pallas kernels for 0%

profile of v1, /device:TPU:0, one launch (start us, length us, event | category | flops | bytes accessed | tf_op | source)
XLA Modules:
  0.0 312.2 jit_solution(12871400326889406711)
XLA Ops:
  3.9 5.0 %collective-permute-start.2 = (bf16[528,128]{1,0:T(8,128)(2,1)}, bf16[528,128]{1,0:T(8,128)(2,1)S(1)}, u32[]{:S(2)}, u32[]{:S(2)}) collective-permute-start(bf16[528,128]{1,0:T(8,128)(2,1)} %get-tuple-element.33), channel_id=1, source_target_pairs={{0,24},{1,25},{2,26},{3,27},{4,28},{5,29},{6,30},{7,31},{8,16},{9,... | collective-permute-start | bytes 405512 | tf_op jit(solution)/shard_map/ppermute | solution.py:24
  9.5 3.8 %collective-permute-start.20 = (bf16[128,1024]{1,0:T(8,128)(2,1)}, bf16[128,1024]{1,0:T(8,128)(2,1)}, u32[]{:S(2)}, u32[]{:S(2)}) collective-permute-start(bf16[128,1024]{1,0:T(8,128)(2,1)} %param.25), channel_id=1, source_target_pairs={{0,24},{1,25},{2,26},{3,27},{4,28},{5,29},{6,30},{7,31},{8,16},{9,... | collective-permute-start | bytes 786440 | tf_op jit(solution)/shard_map/ppermute | solution.py:24
  13.9 1.2 select_reduce_fusion.1
  16.5 1.3 convert_reduce_fusion.1
  17.8 2.2 collective-permute-start.18
  20.0 12.7 %collective-permute-done.1 = bf16[528,128]{1,0:T(8,128)(2,1)S(1)} collective-permute-done((bf16[528,128]{1,0:T(8,128)(2,1)}, bf16[528,128]{1,0:T(8,128)(2,1)S(1)}, u32[]{:S(2)}, u32[]{:S(2)}) %collective-permute-start.1) | collective-permute-done | bytes 135200 | tf_op jit(solution)/shard_map/ppermute | solution.py:24
  32.8 2.0 fusion.125
  34.8 1.5 collective-permute-start.3
  37.7 1.5 compare_and_fusion
  39.1 4.0 %collective-permute-done.19 = bf16[128,1024]{1,0:T(8,128)(2,1)} collective-permute-done((bf16[128,1024]{1,0:T(8,128)(2,1)}, bf16[128,1024]{1,0:T(8,128)(2,1)}, u32[]{:S(2)}, u32[]{:S(2)}) %collective-permute-start.19) | collective-permute-done | bytes 262176 | tf_op jit(solution)/shard_map/ppermute | solution.py:24
  43.2 2.3 pad_maximum_fusion.6
  45.5 1.5 collective-permute-start.21
  47.0 2.5 fusion.124
  50.2 1.6 collective-permute-start.4
  52.7 1.3 eq.57
  54.0 1.3 copy.95
  58.0 11.0 %collective-permute-done.21 = bf16[4,128,1024]{2,1,0:T(8,128)(2,1)} collective-permute-done((bf16[4,128,1024]{2,1,0:T(8,128)(2,1)}, bf16[4,128,1024]{2,1,0:T(8,128)(2,1)}, u32[]{:S(2)}, u32[]{:S(2)}) %collective-permute-start.21) | collective-permute-done | bytes 1048608 | tf_op jit(solution)/shard_map/ppermute | solution.py:24
  69.0 4.7 %fusion.12 = bf16[2,2,2,160,1024]{4,3,1,2,0:T(8,128)(2,1)} fusion(f32[2,2,2,160]{3,1,2,0:T(2,128)S(1)} %copy.106, bf16[1,512,1024]{2,1,0:T(8,128)(2,1)} %bitcast.62, bf16[1,512,1024]{2,1,0:T(8,128)(2,1)} %bitcast.61, s32[2,2,2,512]{3,0,1,2:T(2,128)} %copy.95), kind=kOutput, calls=%fused_computation.20 | convolution fusion | flops 1349648384 | bytes 4740096 | tf_op jit(solution)/shard_map/kearu,aud->keard/dot_general | solution.py:167
  73.6 1.4 pad_maximum_fusion.3
  76.2 7.2 %fusion = (f32[2,8,128]{2,1,0:T(8,128)S(1)}, f32[2,16,128,8,128]{4,2,3,1,0:T(8,128)}) fusion(pred[128,16,128]{0,2,1:T(8,128)(4,1)S(1)} %compare_and_fusion, bf16[128,2,8,128]{3,2,1,0:T(8,128)(2,1)S(1)} %bitcast.258, bf16[16,2,128,128,1]{3,2,1,0,4:T(8,128)(2,1)S(1)} %bitcast.251), kind=kOutput, calls=%fused_computation.2 | convolution fusion | flops 1086322688 | bytes 18620416 | tf_op jit(solution)/shard_map/kgqd,cksd->kgqcs/dot_general | solution.py:122
  83.4 9.1 %fusion.3 = f32[2,8,128]{2,1,0:T(8,128)S(1)} fusion(f32[2,16,128,8,128]{4,2,3,1,0:T(8,128)} %get-tuple-element.39, f32[2,8,128]{2,1,0:T(8,128)S(1)} %get-tuple-element.38, pred[128,16,128]{0,2,1:T(8,128)(4,1)S(1)} %compare_and_fusion), kind=kLoop, calls=%fused_computation.6 | loop fusion | flops 16775168 | bytes 17055744 | tf_op jit(solution)/shard_map/reduce_sum | solution.py:127
  92.5 10.0 %fusion.74 = bf16[128,2,8,128]{0,3,2,1:T(8,128)(2,1)} fusion(f32[2,16,128,8,128]{4,2,3,1,0:T(8,128)} %get-tuple-element.39, f32[2,8,128]{2,1,0:T(8,128)S(1)} %get-tuple-element.38, pred[128,16,128]{0,2,1:T(8,128)(4,1)S(1)} %compare_and_fusion, bf16[16,2,128,128,1]{3,2,1,0,4:T(8,128)(2,1)} %bitcast.257, f32[128,2,8]{0,2,1:T(8,128)S(1)} %bitcast.268), kind=kOutput, calls=%fused_computation.100 | convolution fusion | flops 1091043328 | bytes 18628608 | tf_op jit(solution)/shard_map/kgqcs,cksd->kgqd/dot_general | solution.py:128
  102.6 5.0 %fusion.135 = f32[128,2048]{1,0:T(8,128)S(1)} fusion(bf16[128,2048]{0,1:T(8,128)(2,1)} %bitcast.254, bf16[2048,2048]{1,0:T(8,128)(2,1)} %param.18), kind=kOutput, calls=%fused_computation.205 | convolution fusion | flops 1073741824 | bytes 9961472 | tf_op jit(solution)/shard_map/dot_general | solution.py:132
  107.7 1.8 fusion.130
  109.5 2.5 collective-permute-start.22
  112.2 2.5 psum.14
  114.9 2.7 collective-permute-start.8
  117.6 1.7 collective-permute-start.6
  119.4 6.6 %collective-permute-done.8 = bf16[128,1024]{1,0:T(8,128)(2,1)S(1)} collective-permute-done((bf16[128,1024]{1,0:T(8,128)(2,1)S(1)}, bf16[128,1024]{1,0:T(8,128)(2,1)S(1)}, u32[]{:S(2)}, u32[]{:S(2)}) %collective-permute-start.8) | collective-permute-done | bytes 262176 | tf_op jit(solution)/shard_map/ppermute | solution.py:24
  126.0 13.4 %collective-permute-done.7 = bf16[128,1024]{1,0:T(8,128)(2,1)S(1)} collective-permute-done((bf16[128,1024]{1,0:T(8,128)(2,1)S(1)}, bf16[128,1024]{1,0:T(8,128)(2,1)S(1)}, u32[]{:S(2)}, u32[]{:S(2)}) %collective-permute-start.7) | collective-permute-done | bytes 262176 | tf_op jit(solution)/shard_map/ppermute | solution.py:24
  139.6 1.6 collective-permute-start.9
  141.1 1.6 pad_maximum_fusion.1
  143.1 11.4 %collective-permute-done.9 = bf16[4,128,1024]{2,1,0:T(8,128)(2,1)S(1)} collective-permute-done((bf16[4,128,1024]{2,1,0:T(8,128)(2,1)S(1)}, bf16[4,128,1024]{2,1,0:T(8,128)(2,1)S(1)}, u32[]{:S(2)}, u32[]{:S(2)}) %collective-permute-start.9) | collective-permute-done | bytes 1048608 | tf_op jit(solution)/shard_map/ppermute | solution.py:24
  154.5 1.5 convert_bitcast_fusion
  156.3 1.6 collective-permute-start.10
  157.9 16.1 %collective-permute-done.10 = bf16[2,2,160,1024]{3,2,0,1:T(8,128)(2,1)S(1)} collective-permute-done((bf16[2,2,160,1024]{3,2,0,1:T(8,128)(2,1)S(1)}, bf16[2,2,160,1024]{3,2,0,1:T(8,128)(2,1)S(1)}, u32[]{:S(2)}, u32[]{:S(2)}) %collective-permute-start.10) | collective-permute-done | bytes 1310752 | tf_op jit(solution)/shard_map/ppermute | solution.py:24
  174.7 4.5 %maximum_select_fusion.1 = bf16[2,2,2,160,2048]{4,3,1,2,0:T(8,128)(2,1)S(1)} fusion(bf16[2,2,2,160,1024]{4,3,1,2,0:T(8,128)(2,1)S(1)} %bitcast.252, bf16[1,2,2,160,1024]{4,3,1,2,0:T(8,128)(2,1)} %bitcast.67, bf16[1,2,2,160,1024]{4,3,1,2,0:T(8,128)(2,1)S(1)} %copy-done.1, pred[]{:T(512)S(6)} %eq.25), kind=kLoop, calls=%fused_computation.12 | loop fusion | flops 34078720 | bytes 10485761 | tf_op jit(solution)/shard_map/jit(_where)/select_n | solution.py:174
  179.3 2.9 fusion.15
  182.2 2.0 maximum_select_fusion
  184.3 2.9 fusion.19
  187.1 4.6 %fusion.63 = (bf16[2,2,2,160,384]{4,3,2,0,1:T(8,128)(2,1)}, f32[2,2,2,160,384]{4,3,2,1,0:T(8,128)}) fusion(f32[2,2,2,160,384]{4,3,2,1,0:T(8,128)S(1)} %fusion.19, bf16[2,2048,384]{2,1,0:T(8,128)(2,1)S(1)} %copy-done, bf16[2,2,2,160,2048]{4,3,1,2,0:T(8,128)(2,1)S(1)} %maximum_select_fusion), kind=kOutput, calls=%fused_computation.80 | convolution fusion | flops 2016215040 | bytes 13303808 | tf_op jit(solution)/shard_map/beard,edf->bearf/dot_general | solution.py:205
  191.7 4.7 %fusion.25 = f32[2,2,2,160,2048]{4,3,2,1,0:T(8,128)S(1)} fusion(bf16[2,2048,384]{2,1,0:T(8,128)(2,1)S(1)} %copy-done.6, f32[2,2,2,160,384]{4,3,2,1,0:T(8,128)S(1)} %fusion.15, f32[2,2,2,160,384]{4,3,2,1,0:T(8,128)} %get-tuple-element.41, f32[2,2,2,160,384]{4,3,2,1,0:T(8,128)S(1)} %fusion.19), kind=kOutput, calls=%fused_computation.34 | convolution fusion | flops 2018181120 | bytes 19529728 | tf_op jit(solution)/shard_map/bearf,edf->beard/dot_general | solution.py:219
  196.5 5.8 %convolution_add_fusion = f32[2,2,2,160,2048]{4,3,2,1,0:T(8,128)} fusion(f32[2,2,2,160,2048]{4,3,2,1,0:T(8,128)S(1)} %fusion.25, bf16[2,2048,384]{2,1,0:T(8,128)(2,1)S(1)} %copy-done, f32[2,2,2,160,384]{4,3,2,1,0:T(8,128)S(1)} %fusion.15, f32[2,2,2,160,384]{4,3,2,1,0:T(8,128)S(1)} %fusion.19), kind=kOutput, calls=%fused_computation.27 | convolution fusion | flops 2018836480 | bytes 28049408 | tf_op jit(solution)/shard_map/bearf,edf->beard/dot_general | solution.py:221
  202.3 3.1 fusion.32
  206.0 2.9 fusion.29
  210.6 2.8 fusion.9
  213.7 1.6 collective-permute-start.25
  215.3 2.8 fusion.11
  219.3 12.1 %collective-permute-done.25 = bf16[2,2,160,1024]{3,2,1,0:T(8,128)(2,1)S(1)} collective-permute-done((bf16[2,2,160,1024]{3,2,1,0:T(8,128)(2,1)S(1)}, bf16[2,2,160,1024]{3,2,1,0:T(8,128)(2,1)S(1)}, u32[]{:S(2)}, u32[]{:S(2)}) %collective-permute-start.25) | collective-permute-done | bytes 1310752 | tf_op jit(solution)/shard_map/ppermute | solution.py:24
  231.4 1.9 fusion.44
  233.4 1.6 collective-permute-start.26
  235.0 20.2 %collective-permute-done.13 = bf16[2,2,160,1024]{3,2,1,0:T(8,128)(2,1)S(1)} collective-permute-done((bf16[2,2,160,1024]{3,2,1,0:T(8,128)(2,1)S(1)}, bf16[2,2,160,1024]{3,2,1,0:T(8,128)(2,1)S(1)}, u32[]{:S(2)}, u32[]{:S(2)}) %collective-permute-start.13) | collective-permute-done | bytes 1310752 | tf_op jit(solution)/shard_map/ppermute | solution.py:24
  255.2 3.8 %multiply_reduce_fusion = f32[2,512,1024]{2,1,0:T(8,128)S(1)} fusion(f32[2,2,2,512]{3,2,1,0:T(2,128)S(1)} %copy-done.21, bf16[1,2,2,160,1024]{4,3,2,1,0:T(8,128)(2,1)S(1)} %bitcast.270, bf16[1,2,2,160,1024]{4,3,2,1,0:T(8,128)(2,1)S(1)} %get-tuple-element.14, s32[2,2,2,512]{3,0,1,2:T(2,128)S(1)} %copy-done.19), kind=kOutput, calls=%fused_computation.5 | convolution fusion | flops 1351483392 | bytes 6848512 | tf_op jit(solution)/shard_map/kearu,keard->keaud/dot_general | solution.py:188
  259.2 1.6 collective-permute-start.14
  260.7 4.1 %bitcast_convert_fusion = bf16[2,384,2048]{2,1,0:T(8,128)(2,1)} fusion(bf16[2,2,2,160,2048]{4,3,1,2,0:T(8,128)(2,1)S(1)} %bitcast.248, bf16[2,2,2,160,384]{4,3,2,0,1:T(8,128)(2,1)S(1)} %copy-done.14), kind=kOutput, calls=%fused_computation.10 | convolution fusion | flops 2014838784 | bytes 9371648 | tf_op jit(solution)/shard_map/bearf,beard->efd/dot_general | solution.py:216
  265.3 1.2 collective-permute-start.29
  266.6 3.2 %collective-permute-start.27 = (bf16[128,1024]{1,0:T(8,128)(2,1)S(1)}, bf16[128,1024]{1,0:T(8,128)(2,1)S(1)}, u32[]{:S(2)}, u32[]{:S(2)}) collective-permute-start(bf16[128,1024]{1,0:T(8,128)(2,1)S(1)} %get-tuple-element.22), channel_id=1, source_target_pairs={{0,8},{1,9},{2,10},{3,11},{4,12},{5,13},{6,14},{7,15},{8,0},{9,1},... | collective-permute-start | bytes 786440 | tf_op jit(solution)/shard_map/ppermute | solution.py:24
  269.8 4.3 %collective-permute-done.14 = bf16[512,1024]{1,0:T(8,128)(2,1)S(1)} collective-permute-done((bf16[512,1024]{1,0:T(8,128)(2,1)S(1)}, bf16[512,1024]{1,0:T(8,128)(2,1)S(1)}, u32[]{:S(2)}, u32[]{:S(2)}) %collective-permute-start.14) | collective-permute-done | bytes 1048608 | tf_op jit(solution)/shard_map/ppermute | solution.py:24
  274.0 1.8 fusion.128
  277.9 9.1 %collective-permute-start.15 = (bf16[128,1024]{1,0:T(8,128)(2,1)}, bf16[128,1024]{1,0:T(8,128)(2,1)}, u32[]{:S(2)}, u32[]{:S(2)}) collective-permute-start(bf16[128,1024]{1,0:T(8,128)(2,1)} %get-tuple-element.25), channel_id=1, source_target_pairs={{0,8},{1,9},{2,10},{3,11},{4,12},{5,13},{6,14},{7,15},{8,0},{9,1},... | collective-permute-start | bytes 786440 | tf_op jit(solution)/shard_map/ppermute | solution.py:24
  287.0 13.2 %collective-permute-done.28 = bf16[128,1024]{1,0:T(8,128)(2,1)S(1)} collective-permute-done((bf16[128,1024]{1,0:T(8,128)(2,1)S(1)}, bf16[128,1024]{1,0:T(8,128)(2,1)S(1)}, u32[]{:S(2)}, u32[]{:S(2)}) %collective-permute-start.28) | collective-permute-done | bytes 262176 | tf_op jit(solution)/shard_map/ppermute | solution.py:24
  301.3 2.5 psum.15
  304.2 4.8 %collective-permute-done.16 = bf16[128,1024]{1,0:T(8,128)(2,1)} collective-permute-done((bf16[128,1024]{1,0:T(8,128)(2,1)}, bf16[128,1024]{1,0:T(8,128)(2,1)}, u32[]{:S(2)}, u32[]{:S(2)}) %collective-permute-start.16) | collective-permute-done | bytes 262176 | tf_op jit(solution)/shard_map/ppermute | solution.py:24
  309.0 2.9 fusion.96
  (135 shorter events, 22.8 us)
Async XLA Ops:
  0.6 186.5 %copy-start = (bf16[2,2048,384]{2,1,0:T(8,128)(2,1)S(1)}, bf16[2,2048,384]{2,1,0:T(8,128)(2,1)}, u32[]{:S(2)}) copy-start(bf16[2,2048,384]{2,1,0:T(8,128)(2,1)} %param.23) | copy-start | bytes 9437188
  3.9 13.9 %collective-permute-start.2 = (bf16[528,128]{1,0:T(8,128)(2,1)}, bf16[528,128]{1,0:T(8,128)(2,1)S(1)}, u32[]{:S(2)}, u32[]{:S(2)}) collective-permute-start(bf16[528,128]{1,0:T(8,128)(2,1)} %get-tuple-element.33), channel_id=1, source_target_pairs={{0,24},{1,25},{2,26},{3,27},{4,28},{5,29},{6,30},{7,31},{8,16},{9,... | collective-permute-start | bytes 405512 | tf_op jit(solution)/shard_map/ppermute | solution.py:24
  8.9 23.8 %collective-permute-start.1 = (bf16[528,128]{1,0:T(8,128)(2,1)}, bf16[528,128]{1,0:T(8,128)(2,1)S(1)}, u32[]{:S(2)}, u32[]{:S(2)}) collective-permute-start(bf16[528,128]{1,0:T(8,128)(2,1)} %get-tuple-element.33), channel_id=1, source_target_pairs={{0,16},{1,17},{2,18},{3,19},{4,20},{5,21},{6,22},{7,23},{8,24},{9,... | collective-permute-start | bytes 405512 | tf_op jit(solution)/shard_map/ppermute | solution.py:24
  8.9 23.8 %collective-permute-start = (bf16[528,128]{1,0:T(8,128)(2,1)}, bf16[528,128]{1,0:T(8,128)(2,1)}, u32[]{:S(2)}, u32[]{:S(2)}) collective-permute-start(bf16[528,128]{1,0:T(8,128)(2,1)} %get-tuple-element.33), channel_id=1, source_target_pairs={{0,8},{1,9},{2,10},{3,11},{4,12},{5,13},{6,14},{7,15},{8,0},{9,1},... | collective-permute-start | bytes 405512 | tf_op jit(solution)/shard_map/ppermute | solution.py:24
  9.5 29.6 %collective-permute-start.20 = (bf16[128,1024]{1,0:T(8,128)(2,1)}, bf16[128,1024]{1,0:T(8,128)(2,1)}, u32[]{:S(2)}, u32[]{:S(2)}) collective-permute-start(bf16[128,1024]{1,0:T(8,128)(2,1)} %param.25), channel_id=1, source_target_pairs={{0,24},{1,25},{2,26},{3,27},{4,28},{5,29},{6,30},{7,31},{8,16},{9,... | collective-permute-start | bytes 786440 | tf_op jit(solution)/shard_map/ppermute | solution.py:24
  13.3 29.8 %collective-permute-start.19 = (bf16[128,1024]{1,0:T(8,128)(2,1)}, bf16[128,1024]{1,0:T(8,128)(2,1)}, u32[]{:S(2)}, u32[]{:S(2)}) collective-permute-start(bf16[128,1024]{1,0:T(8,128)(2,1)} %param.25), channel_id=1, source_target_pairs={{0,16},{1,17},{2,18},{3,19},{4,20},{5,21},{6,22},{7,23},{8,24},{9,... | collective-permute-start | bytes 786440 | tf_op jit(solution)/shard_map/ppermute | solution.py:24
  16.5 19.8 %copy-start.17 = (s32[16,128]{1,0:T(8,128)}, s32[16,128]{1,0:T(8,128)S(1)}, u32[]{:S(2)}) copy-start(s32[16,128]{1,0:T(8,128)S(1)} %add_select_fusion) | copy-start | bytes 24580
  16.5 16.3 %copy-start.22 = (s32[128]{0:T(128)}, s32[128]{0:T(128)S(1)}, u32[]{:S(2)}) copy-start(s32[128]{0:T(128)S(1)} %add_select_fusion.1) | copy-start | bytes 1540
  17.8 25.3 %collective-permute-start.18 = (bf16[128,1024]{1,0:T(8,128)(2,1)}, bf16[128,1024]{1,0:T(8,128)(2,1)}, u32[]{:S(2)}, u32[]{:S(2)}) collective-permute-start(bf16[128,1024]{1,0:T(8,128)(2,1)} %param.25), channel_id=1, source_target_pairs={{0,8},{1,9},{2,10},{3,11},{4,12},{5,13},{6,14},{7,15},{8,0},{9,1},... | collective-permute-start | bytes 786440 | tf_op jit(solution)/shard_map/ppermute | solution.py:24
  34.8 12.2 %collective-permute-start.3 = (bf16[4,528,128]{2,1,0:T(8,128)(2,1)}, bf16[4,528,128]{2,1,0:T(8,128)(2,1)}, u32[]{:S(2)}, u32[]{:S(2)}) collective-permute-start(bf16[4,528,128]{2,1,0:T(8,128)(2,1)} %get-tuple-element.29), channel_id=1, source_target_pairs={{0,2},{1,5},{2,0},{3,7},{4,6},{5,1},{6,4},{7,3},{8,10},{9,13},{10,... | collective-permute-start | bytes 1622024 | tf_op jit(solution)/shard_map/ppermute | solution.py:24
  37.7 9.3 %copy-start.3 = (bf16[1,4,528,128]{3,2,1,0:T(8,128)(2,1)S(1)}, bf16[1,4,528,128]{3,2,1,0:T(8,128)(2,1)}, u32[]{:S(2)}) copy-start(bf16[1,4,528,128]{3,2,1,0:T(8,128)(2,1)} %get-tuple-element.28) | copy-start | bytes 1622020
  45.5 23.5 %collective-permute-start.21 = (bf16[4,128,1024]{2,1,0:T(8,128)(2,1)}, bf16[4,128,1024]{2,1,0:T(8,128)(2,1)}, u32[]{:S(2)}, u32[]{:S(2)}) collective-permute-start(bf16[4,128,1024]{2,1,0:T(8,128)(2,1)} %pad_maximum_fusion.6), channel_id=1, source_target_pairs={{0,2},{1,5},{2,0},{3,7},{4,6},{5,1},{6,4},{7,3},{8,10},{9,13},{10,... | collective-permute-start | bytes 3145736 | tf_op jit(solution)/shard_map/ppermute | solution.py:24
  50.2 23.4 %collective-permute-start.4 = (bf16[2,4,528,128]{3,2,1,0:T(8,128)(2,1)}, bf16[2,4,528,128]{3,2,1,0:T(8,128)(2,1)}, u32[]{:S(2)}, u32[]{:S(2)}) collective-permute-start(bf16[2,4,528,128]{3,2,1,0:T(8,128)(2,1)} %get-tuple-element.21), channel_id=1, source_target_pairs={{0,4},{1,3},{2,6},{3,1},{4,0},{5,7},{6,2},{7,5},{8,12},{9,11},{10,... | collective-permute-start | bytes 3244040 | tf_op jit(solution)/shard_map/ppermute | solution.py:24
  56.9 16.7 %copy-start.20 = (f32[2,2,2,512]{3,2,1,0:T(2,128)}, f32[2,2,2,512]{3,2,1,0:T(2,128)S(1)}, u32[]{:S(2)}) copy-start(f32[2,2,2,512]{3,2,1,0:T(2,128)S(1)} %broadcast_divide_fusion) | copy-start | bytes 49156
  69.0 4.7 %copy-start.5 = (bf16[1,2,4,528,128]{4,3,2,1,0:T(8,128)(2,1)S(1)}, bf16[1,2,4,528,128]{4,3,2,1,0:T(8,128)(2,1)}, u32[]{:S(2)}) copy-start(bf16[1,2,4,528,128]{4,3,2,1,0:T(8,128)(2,1)} %get-tuple-element.20) | copy-start | bytes 3244036
  75.1 1.1 copy-start.15
  102.6 5.1 %copy-start.9 = (bf16[2,2,2,160,1024]{4,3,1,2,0:T(8,128)(2,1)S(1)}, bf16[2,2,2,160,1024]{4,3,1,2,0:T(8,128)(2,1)}, u32[]{:S(2)}) copy-start(bf16[2,2,2,160,1024]{4,3,1,2,0:T(8,128)(2,1)} %fusion.12) | copy-start | bytes 7864324
  107.6 4.5 %copy-start.16 = (bf16[128,1024]{1,0:T(8,128)(2,1)S(1)}, bf16[128,1024]{1,0:T(8,128)(2,1)}, u32[]{:S(2)}) copy-start(bf16[128,1024]{1,0:T(8,128)(2,1)} %param.13) | copy-start | bytes 786436
  107.6 4.5 %collective-permute-start.5 = (bf16[128,1024]{1,0:T(8,128)(2,1)S(1)}, bf16[128,1024]{1,0:T(8,128)(2,1)S(1)}, u32[]{:S(2)}, u32[]{:S(2)}) collective-permute-start(bf16[128,1024]{1,0:T(8,128)(2,1)S(1)} %dynamic-slice_convert_fusion.2), channel_id=1, source_target_pairs={{0,1},{1,0},{2,3},{3,2},{4,5},{5,4},{6,7},{7,6},{8,9},{9,8},{10,11... | collective-permute-start | bytes 786440 | tf_op jit(solution)/shard_map/ppermute | solution.py:29
  109.5 31.6 %collective-permute-start.22 = (bf16[2,2,160,1024]{3,2,0,1:T(8,128)(2,1)}, bf16[2,2,160,1024]{3,2,0,1:T(8,128)(2,1)}, u32[]{:S(2)}, u32[]{:S(2)}) collective-permute-start(bf16[2,2,160,1024]{3,2,0,1:T(8,128)(2,1)} %get-tuple-element.13), channel_id=1, source_target_pairs={{0,4},{1,3},{2,6},{3,1},{4,0},{5,7},{6,2},{7,5},{8,12},{9,11},{10,... | collective-permute-start | bytes 3932168 | tf_op jit(solution)/shard_map/ppermute | solution.py:24
  114.7 26.4 %copy-start.1 = (bf16[1,2,2,160,1024]{4,3,1,2,0:T(8,128)(2,1)S(1)}, bf16[1,2,2,160,1024]{4,3,1,2,0:T(8,128)(2,1)}, u32[]{:S(2)}) copy-start(bf16[1,2,2,160,1024]{4,3,1,2,0:T(8,128)(2,1)} %get-tuple-element.12) | copy-start | bytes 3932164
  114.9 11.2 %collective-permute-start.8 = (bf16[128,1024]{1,0:T(8,128)(2,1)S(1)}, bf16[128,1024]{1,0:T(8,128)(2,1)S(1)}, u32[]{:S(2)}, u32[]{:S(2)}) collective-permute-start(bf16[128,1024]{1,0:T(8,128)(2,1)S(1)} %fusion.91), channel_id=1, source_target_pairs={{0,24},{1,25},{2,26},{3,27},{4,28},{5,29},{6,30},{7,31},{8,16},{9,... | collective-permute-start | bytes 786440 | tf_op jit(solution)/shard_map/ppermute | solution.py:24
  117.6 21.8 %collective-permute-start.7 = (bf16[128,1024]{1,0:T(8,128)(2,1)S(1)}, bf16[128,1024]{1,0:T(8,128)(2,1)S(1)}, u32[]{:S(2)}, u32[]{:S(2)}) collective-permute-start(bf16[128,1024]{1,0:T(8,128)(2,1)S(1)} %fusion.91), channel_id=1, source_target_pairs={{0,16},{1,17},{2,18},{3,19},{4,20},{5,21},{6,22},{7,23},{8,24},{9,... | collective-permute-start | bytes 786440 | tf_op jit(solution)/shard_map/ppermute | solution.py:24
  117.6 21.8 %collective-permute-start.6 = (bf16[128,1024]{1,0:T(8,128)(2,1)S(1)}, bf16[128,1024]{1,0:T(8,128)(2,1)S(1)}, u32[]{:S(2)}, u32[]{:S(2)}) collective-permute-start(bf16[128,1024]{1,0:T(8,128)(2,1)S(1)} %fusion.91), channel_id=1, source_target_pairs={{0,8},{1,9},{2,10},{3,11},{4,12},{5,13},{6,14},{7,15},{8,0},{9,1},... | collective-permute-start | bytes 786440 | tf_op jit(solution)/shard_map/ppermute | solution.py:24
  139.6 14.9 %collective-permute-start.9 = (bf16[4,128,1024]{2,1,0:T(8,128)(2,1)S(1)}, bf16[4,128,1024]{2,1,0:T(8,128)(2,1)S(1)}, u32[]{:S(2)}, u32[]{:S(2)}) collective-permute-start(bf16[4,128,1024]{2,1,0:T(8,128)(2,1)S(1)} %pad_maximum_fusion.5), channel_id=1, source_target_pairs={{0,2},{1,5},{2,0},{3,7},{4,6},{5,1},{6,4},{7,3},{8,10},{9,13},{10,... | collective-permute-start | bytes 3145736 | tf_op jit(solution)/shard_map/ppermute | solution.py:24
  142.7 11.7 %copy-start.18 = (s32[2,2,2,512]{3,0,1,2:T(2,128)S(1)}, s32[2,2,2,512]{3,0,1,2:T(2,128)}, u32[]{:S(2)}) copy-start(s32[2,2,2,512]{3,0,1,2:T(2,128)} %copy.95) | copy-start | bytes 49156
  143.0 31.7 %collective-permute-start.23 = (bf16[2,2,2,160,1024]{4,3,1,0,2:T(8,128)(2,1)S(1)}, bf16[2,2,2,160,1024]{4,3,1,0,2:T(8,128)(2,1)S(1)}, u32[]{:S(2)}, u32[]{:S(2)}) collective-permute-start(bf16[2,2,2,160,1024]{4,3,1,0,2:T(8,128)(2,1)S(1)} %copy.107), channel_id=1, source_target_pairs={{0,1},{1,0},{2,3},{3,2},{4,5},{5,4},{6,7},{7,6},{8,9},{9,8},{10,11... | collective-permute-start | bytes 7864328 | tf_op jit(solution)/shard_map/ppermute | solution.py:29
  156.3 17.7 %collective-permute-start.10 = (bf16[2,2,160,1024]{3,2,0,1:T(8,128)(2,1)S(1)}, bf16[2,2,160,1024]{3,2,0,1:T(8,128)(2,1)S(1)}, u32[]{:S(2)}, u32[]{:S(2)}) collective-permute-start(bf16[2,2,160,1024]{3,2,0,1:T(8,128)(2,1)S(1)} %get-tuple-element.17), channel_id=1, source_target_pairs={{0,4},{1,3},{2,6},{3,1},{4,0},{5,7},{6,2},{7,5},{8,12},{9,11},{10,... | collective-permute-start | bytes 3932168 | tf_op jit(solution)/shard_map/ppermute | solution.py:24
  174.6 7.6 %collective-permute-start.11 = (bf16[2,2,2,160,1024]{4,3,1,0,2:T(8,128)(2,1)S(1)}, bf16[2,2,2,160,1024]{4,3,1,0,2:T(8,128)(2,1)S(1)}, u32[]{:S(2)}, u32[]{:S(2)}) collective-permute-start(bf16[2,2,2,160,1024]{4,3,1,0,2:T(8,128)(2,1)S(1)} %copy.98), channel_id=1, source_target_pairs={{0,1},{1,0},{2,3},{3,2},{4,5},{5,4},{6,7},{7,6},{8,9},{9,8},{10,11... | collective-permute-start | bytes 7864328 | tf_op jit(solution)/shard_map/ppermute | solution.py:29
  174.7 4.6 %copy-start.7 = (bf16[2,384,2048]{2,1,0:T(8,128)(2,1)S(1)}, bf16[2,384,2048]{2,1,0:T(8,128)(2,1)}, u32[]{:S(2)}) copy-start(bf16[2,384,2048]{2,1,0:T(8,128)(2,1)} %param.24) | copy-start | bytes 9437188
  179.3 2.9 copy-start.2
  182.2 2.0 copy-start.6
  202.3 3.6 %copy-start.8 = (bf16[2,384,2048]{2,1,0:T(8,128)(2,1)S(1)}, bf16[2,384,2048]{2,1,0:T(8,128)(2,1)}, u32[]{:S(2)}) copy-start(bf16[2,384,2048]{2,1,0:T(8,128)(2,1)} %param.24) | copy-start | bytes 9437188
  202.3 3.7 %copy-start.13 = (bf16[2,2,2,160,384]{4,3,2,0,1:T(8,128)(2,1)S(1)}, bf16[2,2,2,160,384]{4,3,2,0,1:T(8,128)(2,1)}, u32[]{:S(2)}) copy-start(bf16[2,2,2,160,384]{4,3,2,0,1:T(8,128)(2,1)} %get-tuple-element.40) | copy-start | bytes 2949124
  205.4 5.2 %collective-permute-start.24 = (bf16[2,2,2,160,1024]{4,3,0,2,1:T(8,128)(2,1)S(1)}, bf16[2,2,2,160,1024]{4,3,0,2,1:T(8,128)(2,1)}, u32[]{:S(2)}, u32[]{:S(2)}) collective-permute-start(bf16[2,2,2,160,1024]{4,3,0,2,1:T(8,128)(2,1)S(1)} %fusion.32), channel_id=1, source_target_pairs={{0,1},{1,0},{2,3},{3,2},{4,5},{5,4},{6,7},{7,6},{8,9},{9,8},{10,11... | collective-permute-start | bytes 7864328 | tf_op jit(solution)/shard_map/ppermute | solution.py:29
  205.9 4.7 %slice-start = ((s8[10485760]{0:T(1024)(128)(4,1)}), s8[4194304]{0:T(1024)(128)(4,1)S(1)}, s32[]{:S(2)}) async-start(s8[10485760]{0:T(1024)(128)(4,1)} %bitcast.244), calls=%async_computation | async-start | bytes 8388608
  206.0 4.6 %slice-start.1 = ((s8[10485760]{0:T(1024)(128)(4,1)}), s8[4194304]{0:T(1024)(128)(4,1)S(1)}, s32[]{:S(2)}) async-start(s8[10485760]{0:T(1024)(128)(4,1)} %bitcast.244), calls=%async_computation.1 | async-start | bytes 8388608
  206.0 4.6 %slice-start.2 = ((s8[10485760]{0:T(1024)(128)(4,1)}), s8[2097152]{0:T(1024)(128)(4,1)S(1)}, s32[]{:S(2)}) async-start(s8[10485760]{0:T(1024)(128)(4,1)} %bitcast.244), calls=%async_computation.2 | async-start | bytes 4194304
  209.3 6.0 %collective-permute-start.12 = (bf16[2,2,2,160,1024]{4,3,0,2,1:T(8,128)(2,1)S(1)}, bf16[2,2,2,160,1024]{4,3,0,2,1:T(8,128)(2,1)}, u32[]{:S(2)}, u32[]{:S(2)}) collective-permute-start(bf16[2,2,2,160,1024]{4,3,0,2,1:T(8,128)(2,1)S(1)} %fusion.31), channel_id=1, source_target_pairs={{0,1},{1,0},{2,3},{3,2},{4,5},{5,4},{6,7},{7,6},{8,9},{9,8},{10,11... | collective-permute-start | bytes 7864328 | tf_op jit(solution)/shard_map/ppermute | solution.py:29
  213.7 17.7 %collective-permute-start.25 = (bf16[2,2,160,1024]{3,2,1,0:T(8,128)(2,1)S(1)}, bf16[2,2,160,1024]{3,2,1,0:T(8,128)(2,1)S(1)}, u32[]{:S(2)}, u32[]{:S(2)}) collective-permute-start(bf16[2,2,160,1024]{3,2,1,0:T(8,128)(2,1)S(1)} %get-tuple-element.11), channel_id=1, source_target_pairs={{0,4},{1,3},{2,6},{3,1},{4,0},{5,7},{6,2},{7,5},{8,12},{9,11},{10,... | collective-permute-start | bytes 3932168 | tf_op jit(solution)/shard_map/ppermute | solution.py:24
  218.1 13.2 %copy-start.19 = (s32[2,2,2,512]{3,0,1,2:T(2,128)S(1)}, s32[2,2,2,512]{3,0,1,2:T(2,128)}, u32[]{:S(2)}) copy-start(s32[2,2,2,512]{3,0,1,2:T(2,128)} %copy.95) | copy-start | bytes 49156
  218.4 36.7 %collective-permute-start.13 = (bf16[2,2,160,1024]{3,2,1,0:T(8,128)(2,1)S(1)}, bf16[2,2,160,1024]{3,2,1,0:T(8,128)(2,1)S(1)}, u32[]{:S(2)}, u32[]{:S(2)}) collective-permute-start(bf16[2,2,160,1024]{3,2,1,0:T(8,128)(2,1)S(1)} %get-tuple-element.15), channel_id=1, source_target_pairs={{0,4},{1,3},{2,6},{3,1},{4,0},{5,7},{6,2},{7,5},{8,12},{9,11},{10,... | collective-permute-start | bytes 3932168 | tf_op jit(solution)/shard_map/ppermute | solution.py:24
  231.4 23.8 %copy-start.21 = (f32[2,2,2,512]{3,2,1,0:T(2,128)S(1)}, f32[2,2,2,512]{3,2,1,0:T(2,128)}, u32[]{:S(2)}) copy-start(f32[2,2,2,512]{3,2,1,0:T(2,128)} %copy-done.20) | copy-start | bytes 49156
  233.2 27.5 %slice-start.3 = ((s8[5242880]{0:T(1024)(128)(4,1)}), s8[4194304]{0:T(1024)(128)(4,1)S(1)}, s32[]{:S(2)}) async-start(s8[5242880]{0:T(1024)(128)(4,1)} %bitcast.247), calls=%async_computation.3 | async-start | bytes 8388608
  233.4 31.4 %collective-permute-start.26 = (bf16[512,1024]{1,0:T(8,128)(2,1)S(1)}, bf16[512,1024]{1,0:T(8,128)(2,1)S(1)}, u32[]{:S(2)}, u32[]{:S(2)}) collective-permute-start(bf16[512,1024]{1,0:T(8,128)(2,1)S(1)} %fusion.80), channel_id=1, source_target_pairs={{0,2},{1,5},{2,0},{3,7},{4,6},{5,1},{6,4},{7,3},{8,10},{9,13},{10,... | collective-permute-start | bytes 3145736 | tf_op jit(solution)/shard_map/ppermute | solution.py:24
  255.2 5.6 %slice-start.4 = ((s8[5242880]{0:T(1024)(128)(4,1)}), s8[1048576]{0:T(1024)(128)(4,1)S(1)}, s32[]{:S(2)}) async-start(s8[5242880]{0:T(1024)(128)(4,1)} %bitcast.247), calls=%async_computation.4 | async-start | bytes 2097152
  255.2 5.6 %copy-start.14 = (bf16[2,2,2,160,384]{4,3,2,0,1:T(8,128)(2,1)S(1)}, bf16[2,2,2,160,384]{4,3,2,0,1:T(8,128)(2,1)}, u32[]{:S(2)}) copy-start(bf16[2,2,2,160,384]{4,3,2,0,1:T(8,128)(2,1)} %get-tuple-element.40) | copy-start | bytes 2949124
  259.2 14.9 %collective-permute-start.14 = (bf16[512,1024]{1,0:T(8,128)(2,1)S(1)}, bf16[512,1024]{1,0:T(8,128)(2,1)S(1)}, u32[]{:S(2)}, u32[]{:S(2)}) collective-permute-start(bf16[512,1024]{1,0:T(8,128)(2,1)S(1)} %fusion.79), channel_id=1, source_target_pairs={{0,2},{1,5},{2,0},{3,7},{4,6},{5,1},{6,4},{7,3},{8,10},{9,13},{10,... | collective-permute-start | bytes 3145736 | tf_op jit(solution)/shard_map/ppermute | solution.py:24
  265.2 35.0 %copy-start.4 = (f32[512,1024]{1,0:T(8,128)}, f32[512,1024]{1,0:T(8,128)S(1)}, u32[]{:S(2)}) copy-start(f32[512,1024]{1,0:T(8,128)S(1)} %get-tuple-element.5) | copy-start | bytes 6291460
  265.3 12.6 %collective-permute-start.29 = (bf16[128,1024]{1,0:T(8,128)(2,1)S(1)}, bf16[128,1024]{1,0:T(8,128)(2,1)S(1)}, u32[]{:S(2)}, u32[]{:S(2)}) collective-permute-start(bf16[128,1024]{1,0:T(8,128)(2,1)S(1)} %get-tuple-element.23), channel_id=1, source_target_pairs={{0,24},{1,25},{2,26},{3,27},{4,28},{5,29},{6,30},{7,31},{8,16},{9,... | collective-permute-start | bytes 786440 | tf_op jit(solution)/shard_map/ppermute | solution.py:24
  266.5 33.7 %collective-permute-start.28 = (bf16[128,1024]{1,0:T(8,128)(2,1)S(1)}, bf16[128,1024]{1,0:T(8,128)(2,1)S(1)}, u32[]{:S(2)}, u32[]{:S(2)}) collective-permute-start(bf16[128,1024]{1,0:T(8,128)(2,1)S(1)} %get-tuple-element.24), channel_id=1, source_target_pairs={{0,16},{1,17},{2,18},{3,19},{4,20},{5,21},{6,22},{7,23},{8,24},{9,... | collective-permute-start | bytes 786440 | tf_op jit(solution)/shard_map/ppermute | solution.py:24
  266.6 33.7 %collective-permute-start.27 = (bf16[128,1024]{1,0:T(8,128)(2,1)S(1)}, bf16[128,1024]{1,0:T(8,128)(2,1)S(1)}, u32[]{:S(2)}, u32[]{:S(2)}) collective-permute-start(bf16[128,1024]{1,0:T(8,128)(2,1)S(1)} %get-tuple-element.22), channel_id=1, source_target_pairs={{0,8},{1,9},{2,10},{3,11},{4,12},{5,13},{6,14},{7,15},{8,0},{9,1},... | collective-permute-start | bytes 786440 | tf_op jit(solution)/shard_map/ppermute | solution.py:24
  276.7 27.5 %collective-permute-start.17 = (bf16[128,1024]{1,0:T(8,128)(2,1)}, bf16[128,1024]{1,0:T(8,128)(2,1)}, u32[]{:S(2)}, u32[]{:S(2)}) collective-permute-start(bf16[128,1024]{1,0:T(8,128)(2,1)} %get-tuple-element.26), channel_id=1, source_target_pairs={{0,24},{1,25},{2,26},{3,27},{4,28},{5,29},{6,30},{7,31},{8,16},{9,... | collective-permute-start | bytes 786440 | tf_op jit(solution)/shard_map/ppermute | solution.py:24
  277.9 31.1 %collective-permute-start.16 = (bf16[128,1024]{1,0:T(8,128)(2,1)}, bf16[128,1024]{1,0:T(8,128)(2,1)}, u32[]{:S(2)}, u32[]{:S(2)}) collective-permute-start(bf16[128,1024]{1,0:T(8,128)(2,1)} %get-tuple-element.27), channel_id=1, source_target_pairs={{0,16},{1,17},{2,18},{3,19},{4,20},{5,21},{6,22},{7,23},{8,24},{9,... | collective-permute-start | bytes 786440 | tf_op jit(solution)/shard_map/ppermute | solution.py:24
  277.9 22.3 %copy-start.10 = (bf16[128,1024]{1,0:T(8,128)(2,1)}, bf16[128,1024]{1,0:T(8,128)(2,1)S(1)}, u32[]{:S(2)}) copy-start(bf16[128,1024]{1,0:T(8,128)(2,1)S(1)} %collective-permute-done.29) | copy-start | bytes 786436
  277.9 31.1 %collective-permute-start.15 = (bf16[128,1024]{1,0:T(8,128)(2,1)}, bf16[128,1024]{1,0:T(8,128)(2,1)}, u32[]{:S(2)}, u32[]{:S(2)}) collective-permute-start(bf16[128,1024]{1,0:T(8,128)(2,1)} %get-tuple-element.25), channel_id=1, source_target_pairs={{0,8},{1,9},{2,10},{3,11},{4,12},{5,13},{6,14},{7,15},{8,0},{9,1},... | collective-permute-start | bytes 786440 | tf_op jit(solution)/shard_map/ppermute | solution.py:24
  300.2 0.7 copy-start.11
  300.2 0.8 copy-start.12
